TPU v7x, 512 devices: a whole 4x8x8 slice. The times are simulated.
512 devices in a mesh: cam: 32 (over z_hi, x, core), seq: 16 (over y, z_lo).
Axes of the slice: x: 4, y: 8, z: 8 (z_hi: 4, z_lo: 2; z = z_hi * 2 + z_lo), core: 2. Of those that a mesh axis runs over, the one named last changes fastest.
Arguments:
- cross_queries: bfloat16 [32, 4, 512, 2048], P('cam', None, 'seq'), may hold values from -6 to 6
- cross_keys: bfloat16 [32, 4, 512, 2048], P('cam', None, 'seq'), may hold values from -6 to 6
- cross_values: bfloat16 [32, 4, 512, 2048], P('cam', None, 'seq'), may hold values from -6 to 6
- cached_cross: bfloat16 [32, 4, 512, 2048], P('cam', None, 'seq'), may hold values from -6 to 6
- time_queries: bfloat16 [32, 4, 512, 2048], P('cam', None, 'seq'), may hold values from -6 to 6
- time_keys: bfloat16 [32, 4, 512, 2048], P('cam', None, 'seq'), may hold values from -6 to 6
- refresh: int32 [32, 4, 4], P('cam'), may hold values from 0 to 1, as said below
- neighbours: int32 [32, 2], P('cam'), may hold values from 0 to 31, as said below
- view_bias: float32 [3, 16], replicated, may hold values from -1.5 to 1.5
Outputs:
- block_out: bfloat16 [32, 4, 512, 2048], P('cam', None, 'seq')
Inputs may be any that keep to these rules, and one draw needn't show every extreme that they name: `refresh`: 1 where the block of 128 positions of that camera and frame is refreshed, 0 where its cached result stands. `neighbours`: row c holds (c - 1) mod 32 and (c + 1) mod 32, in either order.
All inputs are finite; a program needn't handle non-finite values.
Results may differ from a plain program's by a relative error of at most 0.012.
Values may be sent and summed in bfloat16 or wider, within the bound.
A program may use at most 64 MiB of HBM per device.

v0:
```python
from functools import reduce
import math

import jax
import jax.numpy as jnp
from jax import lax
from jax.sharding import PartitionSpec as P

HEADS = 16
HEAD_DIM = 128
BLOCK_ROWS = 128


def from_behind(block, axis, distance):
    devices = range(lax.axis_size(axis))
    route = [((i - distance) % len(devices), i) for i in devices]
    return lax.ppermute(block, axis, route)


def cross_frame(query_frame, key_sets, value_sets, head_biases, score_scale):
    score_sets = [
        jnp.einsum("shd,thd->hst", query_frame, key_set, preferred_element_type=jnp.float32)
        * score_scale
        + head_bias[:, None, None]
        for key_set, head_bias in zip(key_sets, head_biases)
    ]
    row_max = reduce(
        jnp.maximum, [jnp.max(score_block, axis=-1, keepdims=True) for score_block in score_sets]
    )
    power_sets = [jnp.exp(score_block - row_max) for score_block in score_sets]
    row_total = reduce(
        jnp.add, [jnp.sum(power_block, axis=-1, keepdims=True) for power_block in power_sets]
    )
    partial_sums = [
        jnp.einsum(
            "hst,thd->shd",
            (power_block / row_total).astype(jnp.bfloat16),
            value_set,
            preferred_element_type=jnp.float32,
        )
        for power_block, value_set in zip(power_sets, value_sets)
    ]
    return reduce(jnp.add, partial_sums).astype(jnp.bfloat16)


def temporal(time_q, time_k, mixed_rows, head_count, score_scale):
    frame_count, row_count, row_width = time_q.shape
    head_size = row_width // head_count
    shape4 = (frame_count, row_count * head_count, head_size)
    query_rows = time_q.astype(jnp.float32)
    key_rows = time_k.astype(jnp.float32)
    time_scores = jnp.sum(query_rows[:, None] * key_rows[None], axis=-1) * score_scale
    score_max = jnp.max(time_scores, axis=1, keepdims=True)
    powers = jnp.exp(time_scores - score_max)
    time_weights = (powers / jnp.sum(powers, axis=1, keepdims=True)).astype(jnp.bfloat16)
    value_rows = mixed_rows.astype(jnp.float32)
    result = jnp.sum(time_weights.astype(jnp.float32)[:, :, :, None] * value_rows[None], axis=1)
    return result.astype(jnp.bfloat16)


def local(
    cross_queries,
    cross_keys,
    cross_values,
    cached_cross,
    time_queries,
    time_keys,
    refresh,
    neighbours,
    view_bias,
):
    frame_count = cross_queries.shape[1]
    pos_dev = cross_queries.shape[2]
    seq_count = lax.axis_size("seq")
    cam_count = lax.axis_size("cam")
    seq_index = lax.axis_index("seq")
    cam_index = lax.axis_index("cam")
    local_heads = HEADS // seq_count
    positions = pos_dev * seq_count
    score_scale = 1.0 / math.sqrt(HEAD_DIM)
    slab_q = cross_queries[0]
    slab_k = cross_keys[0]
    slab_v = cross_values[0]
    slab_cache = cached_cross[0]
    slab_tq = time_queries[0]
    slab_tk = time_keys[0]
    block_flags = refresh[0]
    head_q, head_k, head_v, head_tq, head_tk, head_cache = (
        lax.all_to_all(slab_q, "seq", split_axis=2, concat_axis=1, tiled=True),
        lax.all_to_all(slab_k, "seq", split_axis=2, concat_axis=1, tiled=True),
        lax.all_to_all(slab_v, "seq", split_axis=2, concat_axis=1, tiled=True),
        lax.all_to_all(slab_tq, "seq", split_axis=2, concat_axis=1, tiled=True),
        lax.all_to_all(slab_tk, "seq", split_axis=2, concat_axis=1, tiled=True),
        lax.all_to_all(slab_cache, "seq", split_axis=2, concat_axis=1, tiled=True),
    )
    left_keys, left_values = from_behind((head_k, head_v), "cam", 1)
    right_keys, right_values = from_behind((head_k, head_v), "cam", -1)
    local_bias = lax.dynamic_slice_in_dim(view_bias, seq_index * local_heads, local_heads, 1)
    left_first = neighbours[0, 0] == (cam_index + cam_count - 1) % cam_count
    bias_left = jnp.where(left_first, local_bias[1], local_bias[2])
    bias_right = jnp.where(left_first, local_bias[2], local_bias[1])

    def frame_work(frame_id):

        def select_frame(array):
            return lax.dynamic_index_in_dim(array, frame_id, 0, keepdims=False).reshape(
                positions, local_heads, HEAD_DIM
            )

        result = cross_frame(
            select_frame(head_q),
            (select_frame(head_k), select_frame(left_keys), select_frame(right_keys)),
            (select_frame(head_v), select_frame(left_values), select_frame(right_values)),
            (local_bias[0], bias_left, bias_right),
            score_scale,
        )
        return result.reshape(positions, local_heads * HEAD_DIM)

    cross_out = lax.map(frame_work, jnp.arange(frame_count))
    refresh_flags = jnp.repeat(block_flags, BLOCK_ROWS, axis=1)
    mixed_rows = jnp.where(refresh_flags[:, :, None] == 1, cross_out, head_cache)
    head_result = temporal(head_tq, head_tk, mixed_rows, local_heads, score_scale)
    result = lax.all_to_all(head_result, "seq", split_axis=1, concat_axis=2, tiled=True)
    return result[None]


def solution(mesh):
    in_specs = (
        P("cam", None, "seq", None),
        P("cam", None, "seq", None),
        P("cam", None, "seq", None),
        P("cam", None, "seq", None),
        P("cam", None, "seq", None),
        P("cam", None, "seq", None),
        P("cam", None, None),
        P("cam", None),
        P(),
    )
    out_specs = P("cam", None, "seq", None)
    return jax.shard_map(local, mesh=mesh, in_specs=in_specs, out_specs=out_specs, check_vma=False)
```

profile of v0, /device:TPU:8, one launch (start us, length us, event | category | flops | bytes accessed | tf_op | source)
XLA Modules:
  0.0 240.4 jit_solution(14465316846630551989)
XLA Ops:
  0.0 4.0 %copy.79 = bf16[1,4,32,2048]{2,1,3,0:T(4,128)(2,1)} copy(bf16[1,4,32,2048]{3,2,1,0:T(8,128)(2,1)} %param.12) | data formatting | bytes 1048576 | tf_op args[1]
  6.0 2.7 %reshape.182 = bf16[16,2,8192]{2,1,0:T(2,128)(2,1)} reshape(bf16[2048,4,32]{2,1,0:T(4,128)(2,1)S(1)} %bitcast_bitcast_fusion.3) | data formatting | bytes 1048576
  8.7 9.4 %all-to-all-start.4 = ((bf16[16,2,8192]{2,1,0:T(2,128)(2,1)}), bf16[16,2,8192]{2,1,0:T(2,128)(2,1)S(1)}, u32[]{:S(2)}, u32[]{:S(2)}) async-start(bf16[16,2,8192]{2,1,0:T(2,128)(2,1)} %reshape.182), calls=%async_computation.4 | async-start | bytes 1048576 | tf_op jit(solution)/shard_map/all_to_all | solution.py:90
  18.0 2.5 %copy.75 = bf16[1,4,32,2048]{2,1,3,0:T(4,128)(2,1)} copy(bf16[1,4,32,2048]{3,2,1,0:T(8,128)(2,1)S(1)} %copy-done.8) | data formatting | bytes 1048576 | tf_op args[2]
  22.5 2.7 %reshape.178 = bf16[16,2,8192]{2,1,0:T(2,128)(2,1)} reshape(bf16[2048,4,32]{2,1,0:T(4,128)(2,1)S(1)} %bitcast_bitcast_fusion.5) | data formatting | bytes 1048576
  25.2 7.9 %all-to-all-done.4 = bf16[16,2,8192]{2,1,0:T(2,128)(2,1)S(1)} async-done(((bf16[16,2,8192]{2,1,0:T(2,128)(2,1)}), bf16[16,2,8192]{2,1,0:T(2,128)(2,1)S(1)}, u32[]{:S(2)}, u32[]{:S(2)}) %all-to-all-start.4) | async-done | bytes 524320 | tf_op jit(solution)/shard_map/all_to_all | solution.py:90
  33.1 5.6 %all-to-all-start.2 = ((bf16[16,2,8192]{2,1,0:T(2,128)(2,1)}), bf16[16,2,8192]{2,1,0:T(2,128)(2,1)S(1)}, u32[]{:S(2)}, u32[]{:S(2)}) async-start(bf16[16,2,8192]{2,1,0:T(2,128)(2,1)} %reshape.178), calls=%async_computation.2 | async-start | bytes 1048576 | tf_op jit(solution)/shard_map/all_to_all | solution.py:91
  38.7 3.9 %copy.77 = bf16[1,4,32,2048]{2,1,3,0:T(4,128)(2,1)} copy(bf16[1,4,32,2048]{3,2,1,0:T(8,128)(2,1)} %param.11) | data formatting | bytes 1048576 | tf_op args[0]
  44.6 2.7 %reshape.180 = bf16[16,2,8192]{2,1,0:T(2,128)(2,1)} reshape(bf16[2048,4,32]{2,1,0:T(4,128)(2,1)S(1)} %bitcast_bitcast_fusion.4) | data formatting | bytes 1048576
  47.3 6.1 %all-to-all-done.2 = bf16[16,2,8192]{2,1,0:T(2,128)(2,1)S(1)} async-done(((bf16[16,2,8192]{2,1,0:T(2,128)(2,1)}), bf16[16,2,8192]{2,1,0:T(2,128)(2,1)S(1)}, u32[]{:S(2)}, u32[]{:S(2)}) %all-to-all-start.2) | async-done | bytes 524320 | tf_op jit(solution)/shard_map/all_to_all | solution.py:91
  54.2 5.7 %all-to-all-start.3 = ((bf16[16,2,8192]{2,1,0:T(2,128)(2,1)}), bf16[16,2,8192]{2,1,0:T(2,128)(2,1)S(1)}, u32[]{:S(2)}, u32[]{:S(2)}) async-start(bf16[16,2,8192]{2,1,0:T(2,128)(2,1)} %reshape.180), calls=%async_computation.3 | async-start | bytes 1048576 | tf_op jit(solution)/shard_map/all_to_all | solution.py:89
  59.9 3.9 %copy.69 = bf16[1,4,32,2048]{2,1,3,0:T(4,128)(2,1)} copy(bf16[1,4,32,2048]{3,2,1,0:T(8,128)(2,1)} %param.15) | data formatting | bytes 1048576 | tf_op args[4]
  65.9 2.7 %reshape.188 = bf16[16,2,8192]{2,1,0:T(2,128)(2,1)} reshape(bf16[2048,4,32]{2,1,0:T(4,128)(2,1)S(1)} %bitcast_bitcast_fusion.7) | data formatting | bytes 1048576
  68.6 6.3 %all-to-all-done.3 = bf16[16,2,8192]{2,1,0:T(2,128)(2,1)S(1)} async-done(((bf16[16,2,8192]{2,1,0:T(2,128)(2,1)}), bf16[16,2,8192]{2,1,0:T(2,128)(2,1)S(1)}, u32[]{:S(2)}, u32[]{:S(2)}) %all-to-all-start.3) | async-done | bytes 524320 | tf_op jit(solution)/shard_map/all_to_all | solution.py:89
  74.8 6.1 %all-to-all-start = ((bf16[16,2,8192]{2,1,0:T(2,128)(2,1)}), bf16[16,2,8192]{2,1,0:T(2,128)(2,1)}, u32[]{:S(2)}, u32[]{:S(2)}) async-start(bf16[16,2,8192]{2,1,0:T(2,128)(2,1)} %reshape.188), calls=%async_computation | async-start | bytes 1048576 | tf_op jit(solution)/shard_map/all_to_all | solution.py:92
  80.9 3.9 %copy.72 = bf16[1,4,32,2048]{2,1,3,0:T(4,128)(2,1)} copy(bf16[1,4,32,2048]{3,2,1,0:T(8,128)(2,1)} %param.16) | data formatting | bytes 1048576 | tf_op args[5]
  86.9 2.7 %reshape.186 = bf16[16,2,8192]{2,1,0:T(2,128)(2,1)} reshape(bf16[2048,4,32]{2,1,0:T(4,128)(2,1)S(1)} %bitcast_bitcast_fusion.6) | data formatting | bytes 1048576
  89.6 6.1 %all-to-all-done = bf16[16,2,8192]{2,1,0:T(2,128)(2,1)} async-done(((bf16[16,2,8192]{2,1,0:T(2,128)(2,1)}), bf16[16,2,8192]{2,1,0:T(2,128)(2,1)}, u32[]{:S(2)}, u32[]{:S(2)}) %all-to-all-start) | async-done | bytes 524320 | tf_op jit(solution)/shard_map/all_to_all | solution.py:92
  95.8 5.2 %all-to-all-start.1 = ((bf16[16,2,8192]{2,1,0:T(2,128)(2,1)}), bf16[16,2,8192]{2,1,0:T(2,128)(2,1)S(1)}, u32[]{:S(2)}, u32[]{:S(2)}) async-start(bf16[16,2,8192]{2,1,0:T(2,128)(2,1)} %reshape.186), calls=%async_computation.1 | async-start | bytes 1048576 | tf_op jit(solution)/shard_map/all_to_all | solution.py:93
  104.2 4.0 %copy.82 = bf16[1,4,32,2048]{2,1,3,0:T(4,128)(2,1)} copy(bf16[1,4,32,2048]{3,2,1,0:T(8,128)(2,1)} %param.14) | data formatting | bytes 1048576 | tf_op args[3]
  110.2 2.7 %reshape.184 = bf16[16,2,8192]{2,1,0:T(2,128)(2,1)} reshape(bf16[2048,4,32]{2,1,0:T(4,128)(2,1)S(1)} %bitcast_bitcast_fusion.2) | data formatting | bytes 1048576
  114.8 6.3 %all-to-all-start.5 = ((bf16[16,2,8192]{2,1,0:T(2,128)(2,1)}), bf16[16,2,8192]{2,1,0:T(2,128)(2,1)}, u32[]{:S(2)}, u32[]{:S(2)}) async-start(bf16[16,2,8192]{2,1,0:T(2,128)(2,1)} %reshape.184), calls=%async_computation.5 | async-start | bytes 1048576 | tf_op jit(solution)/shard_map/all_to_all | solution.py:94
  126.6 8.4 %collective-permute-start.1 = (bf16[4,512,128]{2,1,0:T(8,128)(2,1)}, bf16[4,512,128]{2,1,0:T(8,128)(2,1)}, u32[]{:S(2)}, u32[]{:S(2)}) collective-permute-start(bf16[4,512,128]{2,1,0:T(8,128)(2,1)} %bitcast.32), channel_id=1, source_target_pairs={{16,0},{32,16},{48,32},{64,48},{80,64},{96,80},{112,96},{128,112},... | collective-permute-start | bytes 1572872 | tf_op jit(solution)/shard_map/ppermute | solution.py:17
  136.0 2.2 copy.76
  140.2 7.9 %collective-permute-start.3 = (bf16[4,512,128]{2,1,0:T(8,128)(2,1)}, bf16[4,512,128]{2,1,0:T(8,128)(2,1)}, u32[]{:S(2)}, u32[]{:S(2)}) collective-permute-start(bf16[4,512,128]{2,1,0:T(8,128)(2,1)} %bitcast.24), channel_id=1, source_target_pairs={{16,0},{32,16},{48,32},{64,48},{80,64},{96,80},{112,96},{128,112},... | collective-permute-start | bytes 1572872 | tf_op jit(solution)/shard_map/ppermute | solution.py:17
  148.0 3.6 %reshape.189 = bf16[2048,4,32]{2,1,0:T(4,128)(2,1)S(1)} reshape(bf16[16,2,8192]{2,1,0:T(2,128)(2,1)} %all-to-all-done) | data formatting | bytes 1048576
  151.7 2.2 copy.70
  155.1 3.6 %reshape.187 = bf16[2048,4,32]{2,1,0:T(4,128)(2,1)S(1)} reshape(bf16[16,2,8192]{2,1,0:T(2,128)(2,1)} %copy-done.7) | data formatting | bytes 1048576
  158.7 2.2 copy.73
  166.6 3.6 %reshape.185 = bf16[2048,4,32]{2,1,0:T(4,128)(2,1)S(1)} reshape(bf16[16,2,8192]{2,1,0:T(2,128)(2,1)} %all-to-all-done.5) | data formatting | bytes 1048576
  174.8 42.6 %while.10 = (s32[]{:T(128)}, bf16[4,512,128]{2,1,0:T(8,128)(2,1)S(1)}, s32[4]{0:T(128)S(1)}, bf16[4,512,128]{2,1,0:T(8,128)(2,1)}, bf16[4,512,128]{2,1,0:T(8,128...) while((s32[]{:T(128)}, ...), condition=%wide.region_10.11_spmd, body=%wide.region_3.10_spmd.sunk | while | flops 409140224 | bytes 12368595 | solution.py:119
  219.5 19.6 %all_to_all.105 = bf16[4,512,128]{2,0,1:T(4,128)(2,1)S(1)} all-to-all(bf16[4,512,128]{2,0,1:T(4,128)(2,1)S(1)} %copy.86), channel_id=1, replica_groups=mesh['cam'=32,'seq'=16] {'seq'}, dimensions={1} | all-to-all | bytes 1048576 | tf_op jit(solution)/shard_map/all_to_all | solution.py:123
  (114 shorter events, 72.8 us)
Async XLA Ops:
  0.0 101.0 %copy-start = (f32[3,16]{1,0:T(4,128)S(1)}, f32[3,16]{1,0:T(4,128)}, u32[]{:S(2)}) copy-start(f32[3,16]{1,0:T(4,128)} %param.19) | copy-start | bytes 580
  5.9 12.1 %copy-start.8 = (bf16[1,4,32,2048]{3,2,1,0:T(8,128)(2,1)S(1)}, bf16[1,4,32,2048]{3,2,1,0:T(8,128)(2,1)}, u32[]{:S(2)}) copy-start(bf16[1,4,32,2048]{3,2,1,0:T(8,128)(2,1)} %param.13) | copy-start | bytes 1572868
  8.7 24.4 %all-to-all-start.4 = ((bf16[16,2,8192]{2,1,0:T(2,128)(2,1)}), bf16[16,2,8192]{2,1,0:T(2,128)(2,1)S(1)}, u32[]{:S(2)}, u32[]{:S(2)}) async-start(bf16[16,2,8192]{2,1,0:T(2,128)(2,1)} %reshape.182), calls=%async_computation.4 | async-start | bytes 1048576 | tf_op jit(solution)/shard_map/all_to_all | solution.py:90
  33.1 20.3 %all-to-all-start.2 = ((bf16[16,2,8192]{2,1,0:T(2,128)(2,1)}), bf16[16,2,8192]{2,1,0:T(2,128)(2,1)S(1)}, u32[]{:S(2)}, u32[]{:S(2)}) async-start(bf16[16,2,8192]{2,1,0:T(2,128)(2,1)} %reshape.178), calls=%async_computation.2 | async-start | bytes 1048576 | tf_op jit(solution)/shard_map/all_to_all | solution.py:91
  53.4 0.8 copy-start.5
  54.2 20.6 %all-to-all-start.3 = ((bf16[16,2,8192]{2,1,0:T(2,128)(2,1)}), bf16[16,2,8192]{2,1,0:T(2,128)(2,1)S(1)}, u32[]{:S(2)}, u32[]{:S(2)}) async-start(bf16[16,2,8192]{2,1,0:T(2,128)(2,1)} %reshape.180), calls=%async_computation.3 | async-start | bytes 1048576 | tf_op jit(solution)/shard_map/all_to_all | solution.py:89
  74.8 12.0 %copy-start.3 = (bf16[16,2,8192]{2,1,0:T(2,128)(2,1)}, bf16[16,2,8192]{2,1,0:T(2,128)(2,1)S(1)}, u32[]{:S(2)}) copy-start(bf16[16,2,8192]{2,1,0:T(2,128)(2,1)S(1)} %all-to-all-done.3) | copy-start | bytes 1572868
  74.8 20.9 %all-to-all-start = ((bf16[16,2,8192]{2,1,0:T(2,128)(2,1)}), bf16[16,2,8192]{2,1,0:T(2,128)(2,1)}, u32[]{:S(2)}, u32[]{:S(2)}) async-start(bf16[16,2,8192]{2,1,0:T(2,128)(2,1)} %reshape.188), calls=%async_computation | async-start | bytes 1048576 | tf_op jit(solution)/shard_map/all_to_all | solution.py:92
  86.9 14.3 %copy-start.11 = (s32[1,2]{1,0:T(1,128)S(1)}, s32[1,2]{1,0:T(1,128)}, u32[]{:S(2)}) copy-start(s32[1,2]{1,0:T(1,128)} %param.18) | copy-start | bytes 28
  95.8 19.0 %all-to-all-start.1 = ((bf16[16,2,8192]{2,1,0:T(2,128)(2,1)}), bf16[16,2,8192]{2,1,0:T(2,128)(2,1)S(1)}, u32[]{:S(2)}, u32[]{:S(2)}) async-start(bf16[16,2,8192]{2,1,0:T(2,128)(2,1)} %reshape.186), calls=%async_computation.1 | async-start | bytes 1048576 | tf_op jit(solution)/shard_map/all_to_all | solution.py:93
  110.2 10.9 %copy-start.10 = (s32[1,4,4]{2,1,0:T(4,128)S(1)}, s32[1,4,4]{2,1,0:T(4,128)}, u32[]{:S(2)}) copy-start(s32[1,4,4]{2,1,0:T(4,128)} %param.17) | copy-start | bytes 196
  114.8 6.4 %copy-start.7 = (bf16[16,2,8192]{2,1,0:T(2,128)(2,1)}, bf16[16,2,8192]{2,1,0:T(2,128)(2,1)S(1)}, u32[]{:S(2)}) copy-start(bf16[16,2,8192]{2,1,0:T(2,128)(2,1)S(1)} %all-to-all-done.1) | copy-start | bytes 1572868
  114.8 51.8 %all-to-all-start.5 = ((bf16[16,2,8192]{2,1,0:T(2,128)(2,1)}), bf16[16,2,8192]{2,1,0:T(2,128)(2,1)}, u32[]{:S(2)}, u32[]{:S(2)}) async-start(bf16[16,2,8192]{2,1,0:T(2,128)(2,1)} %reshape.184), calls=%async_computation.5 | async-start | bytes 1048576 | tf_op jit(solution)/shard_map/all_to_all | solution.py:94
  121.2 13.7 %copy-start.6 = (bf16[16,2,8192]{2,1,0:T(2,128)(2,1)S(1)}, bf16[16,2,8192]{2,1,0:T(2,128)(2,1)}, u32[]{:S(2)}) copy-start(bf16[16,2,8192]{2,1,0:T(2,128)(2,1)} %copy-done.5) | copy-start | bytes 1572868
  124.5 50.2 %collective-permute-start = (bf16[4,512,128]{2,1,0:T(8,128)(2,1)}, bf16[4,512,128]{2,1,0:T(8,128)(2,1)}, u32[]{:S(2)}, u32[]{:S(2)}) collective-permute-start(bf16[4,512,128]{2,1,0:T(8,128)(2,1)} %bitcast.32), channel_id=1, source_target_pairs={{496,0},{0,16},{16,32},{32,48},{48,64},{64,80},{80,96},{96,112},{1... | collective-permute-start | bytes 1572872 | tf_op jit(solution)/shard_map/ppermute | solution.py:17
  126.6 48.1 %collective-permute-start.1 = (bf16[4,512,128]{2,1,0:T(8,128)(2,1)}, bf16[4,512,128]{2,1,0:T(8,128)(2,1)}, u32[]{:S(2)}, u32[]{:S(2)}) collective-permute-start(bf16[4,512,128]{2,1,0:T(8,128)(2,1)} %bitcast.32), channel_id=1, source_target_pairs={{16,0},{32,16},{48,32},{64,48},{80,64},{96,80},{112,96},{128,112},... | collective-permute-start | bytes 1572872 | tf_op jit(solution)/shard_map/ppermute | solution.py:17
  138.2 36.5 %collective-permute-start.2 = (bf16[4,512,128]{2,1,0:T(8,128)(2,1)}, bf16[4,512,128]{2,1,0:T(8,128)(2,1)}, u32[]{:S(2)}, u32[]{:S(2)}) collective-permute-start(bf16[4,512,128]{2,1,0:T(8,128)(2,1)} %bitcast.24), channel_id=1, source_target_pairs={{496,0},{0,16},{16,32},{32,48},{48,64},{64,80},{80,96},{96,112},{1... | collective-permute-start | bytes 1572872 | tf_op jit(solution)/shard_map/ppermute | solution.py:17
  140.2 34.6 %collective-permute-start.3 = (bf16[4,512,128]{2,1,0:T(8,128)(2,1)}, bf16[4,512,128]{2,1,0:T(8,128)(2,1)}, u32[]{:S(2)}, u32[]{:S(2)}) collective-permute-start(bf16[4,512,128]{2,1,0:T(8,128)(2,1)} %bitcast.24), channel_id=1, source_target_pairs={{16,0},{32,16},{48,32},{64,48},{80,64},{96,80},{112,96},{128,112},... | collective-permute-start | bytes 1572872 | tf_op jit(solution)/shard_map/ppermute | solution.py:17
  162.1 2.1 copy-start.4
  171.5 1.7 copy-start.2
  173.1 1.6 copy-start.9
  219.1 21.3 %copy-start.1 = (f32[3,16]{1,0:T(4,128)S(1)}, f32[3,16]{1,0:T(4,128)}, u32[]{:S(2)}) copy-start(f32[3,16]{1,0:T(4,128)} %param.19) | copy-start | bytes 580
where the time goes:
time: 243 us; the launch traced here: 240 us
  local copies, waits for them, and re-layouts  88.6 us (36%)
  starting transfers between devices  58.5 us (24%)
  matrix products  29.8 us (12%)
  waiting for transfers between devices  28.3 us (12%)
  blocking collectives  19.6 us (8%)
  loops' own time  8.1 us (3%)
  other arithmetic  4.73 us (2%)
  between operations  2.84 us (1%)
    unnamed x53, local copies, waits for them, and re-layouts  67.8 us
    ppermute x4, starting transfers between devices, from_behind(): return lax.ppermute(block, axis, route)  20.2 us
    all_to_all x1, blocking collectives, local(): lax.all_to_all(head_result, 'seq', split_axis=1, concat_axis=2, tiled=True)  19.6 us
    dot_general x12, matrix products, cross_frame(): jnp.einsum('hst,thd->shd', (power_block / row_total).astype(jnp.bfloat16)...  15 us
    dot_general x12, matrix products, cross_frame(): jnp.einsum('shd,thd->hst', query_frame, key_set, preferred_element_type=j...  14.8 us
    all_to_all x1, starting transfers between devices, local(): lax.all_to_all(slab_k, 'seq', split_axis=2, concat_axis=1, tiled=True)  9.37 us
    another operation x1, loops' own time, local(): cross_out = lax.map(frame_work, jnp.arange(frame_count))  8.1 us
    all_to_all x1, waiting for transfers between devices, local(): lax.all_to_all(slab_k, 'seq', split_axis=2, concat_axis=1, tiled=True)  7.88 us
  transfers between devices with their start and end apart: 10, of which 5 were waited for; matrix products, arithmetic and copies ran while one was open for 31% of the time, Pallas kernels for 0%

commit v1 on v0

v1 whole, which is shorter than its diff:
```python
import math

import jax
import jax.numpy as jnp
from jax import lax
from jax.experimental import pallas as pl
from jax.experimental.pallas import tpu as pltpu
from jax.sharding import PartitionSpec as P

HEAD_DIM = 128
BLOCK_ROWS = 128
FRAMES = 4
TILE = 128
LOG2E = math.log2(math.e)
MESH = pl.DeviceIdType.MESH


def kernel(
    refresh_ref,
    neighbours_ref,
    bias_ref,
    q_hbm,
    k_hbm,
    v_hbm,
    cached_hbm,
    tq_hbm,
    tk_hbm,
    out_ref,
    kv,
    qb,
    ob,
    mix,
    local3,
    weights,
    in_sem,
    cam_sem,
    back_sem,
    send_sem,
    local_sem,
):
    seq = lax.axis_index("seq")
    cam = lax.axis_index("cam")
    peers = lax.axis_size("seq")
    cams = lax.axis_size("cam")
    rows = q_hbm.shape[2]
    left = lax.rem(cam + cams - 1, cams)
    right = lax.rem(cam + 1, cams)
    blk = lax.div(seq * rows, BLOCK_ROWS)

    barrier = pltpu.get_barrier_semaphore()

    def greet(i, carry):
        pl.semaphore_signal(
            barrier, inc=1, device_id={"seq": lax.rem(seq + i, peers)}, device_id_type=MESH
        )
        return carry

    lax.fori_loop(1, peers, greet, 0)
    for other in (left, right):
        pl.semaphore_signal(barrier, inc=1, device_id={"cam": other}, device_id_type=MESH)
    pl.semaphore_wait(barrier, peers + 1)

    sources = (k_hbm, v_hbm, q_hbm)
    places = (kv.at[0, 0], kv.at[1, 0], qb)

    def head_cols(index):
        return pl.ds(pl.multiple_of(index * HEAD_DIM, HEAD_DIM), HEAD_DIM)

    def my_rows(index):
        return pl.ds(pl.multiple_of(index * rows, rows), rows)

    def scatter(f):
        for a in range(3):

            def send(i, carry):
                peer = lax.rem(seq + i, peers)
                pltpu.make_async_remote_copy(
                    src_ref=sources[a].at[0, f, :, head_cols(peer)],
                    dst_ref=places[a].at[f, my_rows(seq)],
                    send_sem=send_sem.at[a],
                    recv_sem=in_sem.at[a, f],
                    device_id={"seq": peer},
                    device_id_type=MESH,
                ).start()
                return carry

            lax.fori_loop(1, peers, send, 0)
            pltpu.make_async_copy(
                sources[a].at[0, f, :, head_cols(seq)],
                places[a].at[f, my_rows(seq)],
                in_sem.at[a, f],
            ).start()

    def wait_in(a, f):
        pltpu.make_async_copy(places[a].at[f], places[a].at[f], in_sem.at[a, f]).wait()

    def forward(a, f):
        for slot, other in ((1, right), (2, left)):
            pltpu.make_async_remote_copy(
                src_ref=kv.at[a, 0, f],
                dst_ref=kv.at[a, slot, f],
                send_sem=send_sem.at[3],
                recv_sem=cam_sem.at[f],
                device_id={"cam": other},
                device_id_type=MESH,
            ).start()

    scale = LOG2E / math.sqrt(HEAD_DIM)
    left_first = neighbours_ref[0, 0] == left
    bias_own = bias_ref[0, seq] * LOG2E
    bias_a = bias_ref[1, seq] * LOG2E
    bias_b = bias_ref[2, seq] * LOG2E
    biases = (
        bias_own,
        jnp.where(left_first, bias_a, bias_b),
        jnp.where(left_first, bias_b, bias_a),
    )

    def attend(f):
        pltpu.make_async_copy(kv.at[:, 1:3, f], kv.at[:, 1:3, f], cam_sem.at[f]).wait()

        def tile_work(t, carry):
            tile = pl.ds(pl.multiple_of(t * TILE, TILE), TILE)
            query = qb[f, tile]
            scores = [
                lax.dot_general(
                    query,
                    kv[0, j, f],
                    (((1,), (1,)), ((), ())),
                    preferred_element_type=jnp.float32,
                )
                for j in range(3)
            ]
            tops = [
                jnp.max(s, axis=1, keepdims=True) * scale + b for s, b in zip(scores, biases)
            ]
            top = jnp.maximum(jnp.maximum(tops[0], tops[1]), tops[2])
            total = jnp.zeros((TILE, 1), jnp.float32)
            acc = jnp.zeros((TILE, HEAD_DIM), jnp.float32)
            for j in range(3):
                power = jnp.exp2(scores[j] * scale + (biases[j] - top))
                total = total + jnp.sum(power, axis=1, keepdims=True)
                acc = acc + jnp.dot(
                    power.astype(jnp.bfloat16), kv[1, j, f], preferred_element_type=jnp.float32
                )
            ob[f, tile] = (acc / total).astype(jnp.bfloat16)
            return carry

        lax.fori_loop(0, qb.shape[1] // TILE, tile_work, 0)

        def give_back(i, carry):
            peer = lax.rem(seq + i, peers)
            pltpu.make_async_remote_copy(
                src_ref=ob.at[f, my_rows(peer)],
                dst_ref=mix.at[f, :, head_cols(seq)],
                send_sem=send_sem.at[4],
                recv_sem=back_sem.at[f],
                device_id={"seq": peer},
                device_id_type=MESH,
            ).start()
            return carry

        lax.fori_loop(1, peers, give_back, 0)
        pltpu.make_async_copy(
            ob.at[f, my_rows(seq)], mix.at[f, :, head_cols(seq)], back_sem.at[f]
        ).start()

    def time_weights(h, carry):
        cols = head_cols(h)
        keys = [local3[2, g, :, cols].astype(jnp.float32) for g in range(FRAMES)]
        for f in range(FRAMES):
            query = local3[1, f, :, cols].astype(jnp.float32)
            scores = [jnp.sum(query * key, axis=1, keepdims=True) * scale for key in keys]
            top = scores[0]
            for s in scores[1:]:
                top = jnp.maximum(top, s)
            powers = [jnp.exp2(s - top) for s in scores]
            total = powers[0] + powers[1] + powers[2] + powers[3]
            for g in range(FRAMES):
                weights[f, g, :, cols] = jnp.broadcast_to(
                    (powers[g] / total).astype(jnp.bfloat16), (rows, HEAD_DIM)
                )
        return carry

    scatter(0)
    scatter(1)
    own_rows = [
        pltpu.make_async_copy(src.at[0], local3.at[n], local_sem.at[n])
        for n, src in enumerate((cached_hbm, tq_hbm, tk_hbm))
    ]
    for copy in own_rows:
        copy.start()
    for copy in own_rows:
        copy.wait()
    lax.fori_loop(0, peers, time_weights, 0)

    for f in range(FRAMES):
        wait_in(0, f)
        forward(0, f)
        wait_in(1, f)
        forward(1, f)
        wait_in(2, f)
        if f + 2 < FRAMES:
            scatter(f + 2)
        if f > 0:
            attend(f - 1)
    attend(FRAMES - 1)

    for f in range(FRAMES):
        pltpu.make_async_copy(mix.at[f], mix.at[f], back_sem.at[f]).wait()

    flags = [refresh_ref[0, g, blk] == 1 for g in range(FRAMES)]

    def combine(h, carry):
        cols = head_cols(h)
        mixed = [
            jnp.where(flags[g], mix[g, :, cols], local3[0, g, :, cols]).astype(jnp.float32)
            for g in range(FRAMES)
        ]
        for f in range(FRAMES):
            acc = weights[f, 0, :, cols].astype(jnp.float32) * mixed[0]
            for g in range(1, FRAMES):
                acc = acc + weights[f, g, :, cols].astype(jnp.float32) * mixed[g]
            out_ref[0, f, :, cols] = acc.astype(jnp.bfloat16)
        return carry

    lax.fori_loop(0, peers, combine, 0)

    received = qb.shape[1] - rows
    for a in range(3):
        sent = kv.at[0, 0, :, pl.ds(0, received)]
        pltpu.make_async_copy(sent, sent, send_sem.at[a]).wait()
    sent = kv.at[:, 1:3]
    pltpu.make_async_copy(sent, sent, send_sem.at[3]).wait()
    sent = ob.at[:, pl.ds(0, received)]
    pltpu.make_async_copy(sent, sent, send_sem.at[4]).wait()


def local(
    cross_queries,
    cross_keys,
    cross_values,
    cached_cross,
    time_queries,
    time_keys,
    refresh,
    neighbours,
    view_bias,
):
    _, frames, rows, inner = cross_queries.shape
    positions = rows * lax.axis_size("seq")
    dtype = jnp.bfloat16
    smem = pl.BlockSpec(memory_space=pltpu.SMEM)
    hbm = pl.BlockSpec(memory_space=pltpu.HBM)
    return pl.pallas_call(
        kernel,
        out_shape=jax.ShapeDtypeStruct(cross_queries.shape, dtype),
        in_specs=[smem] * 3 + [hbm] * 6,
        out_specs=pl.BlockSpec(memory_space=pltpu.VMEM),
        scratch_shapes=[
            pltpu.VMEM((2, 3, frames, positions, HEAD_DIM), dtype),
            pltpu.VMEM((frames, positions, HEAD_DIM), dtype),
            pltpu.VMEM((frames, positions, HEAD_DIM), dtype),
            pltpu.VMEM((frames, rows, inner), dtype),
            pltpu.VMEM((3, frames, rows, inner), dtype),
            pltpu.VMEM((frames, frames, rows, inner), dtype),
            pltpu.SemaphoreType.DMA((3, frames)),
            pltpu.SemaphoreType.DMA((frames,)),
            pltpu.SemaphoreType.DMA((frames,)),
            pltpu.SemaphoreType.DMA((5,)),
            pltpu.SemaphoreType.DMA((3,)),
        ],
        compiler_params=pltpu.CompilerParams(
            collective_id=0, has_side_effects=True, vmem_limit_bytes=60 << 20
        ),
    )(
        refresh,
        neighbours,
        view_bias,
        cross_queries,
        cross_keys,
        cross_values,
        cached_cross,
        time_queries,
        time_keys,
    )


def solution(mesh):
    in_specs = (
        P("cam", None, "seq", None),
        P("cam", None, "seq", None),
        P("cam", None, "seq", None),
        P("cam", None, "seq", None),
        P("cam", None, "seq", None),
        P("cam", None, "seq", None),
        P("cam", None, None),
        P("cam", None),
        P(),
    )
    out_specs = P("cam", None, "seq", None)
    return jax.shard_map(local, mesh=mesh, in_specs=in_specs, out_specs=out_specs, check_vma=False)
```

time: 243 us -> 76.8 us (0.32)
  the two profiles are of different devices: /device:TPU:8 before, /device:TPU:64 now
where the time goes in v1:
time: 76.8 us; the launch traced here: 76.6 us
  Pallas kernels  74.7 us (97%)
  local copies, waits for them, and re-layouts  1.88 us (2%)
    pallas_call x1, Pallas kernels, local(): pl.pallas_call(kernel, out_shape=jax.ShapeDtypeStruct(cross_queries.shape...  74.7 us
    unnamed x1, local copies, waits for them, and re-layouts  1.88 us

profile of v1, /device:TPU:64, one launch (start us, length us, event | category | flops | bytes accessed | tf_op | source)
XLA Modules:
  0.0 76.6 jit_solution(5156193229322278974)
XLA Ops:
  0.0 74.7 %shard_map.91 = bf16[1,4,32,2048]{3,2,1,0:T(8,128)(2,1)} custom-call(s32[1,4,4]{2,1,0:T(4,128)} %refresh_ref.1, s32[1,2]{1,0:T(1,128)} %neighbours_ref.1, f32[3,16]{1,0:T(4,128)} %bias_ref.1, bf16[1,4,32,2048]{3,2,1,0:T(8,128)(2,1)} %q_hbm.1, bf16[1,4,32,2048]{3,2,1,0:T(8,128)(2,1)} %k_hbm.1, bf16[1,4,32,2048]{3,2,1,0:T(8,128)(2,1)} %v_hbm.1, ...), custom_call_target="tpu_custom_call" | custom-call | tf_op jit(solution)/shard_map/pallas_call | solution.py:255
  74.7 1.9 %copy.11 = bf16[1,4,32,2048]{3,2,1,0:T(8,128)(2,1)} copy(bf16[1,4,32,2048]{3,2,1,0:T(8,128)(2,1)} %shard_map.91) | data formatting | bytes 1048576

commit v2 on v1

--- a/solution.py
+++ b/solution.py
@@ -10,6 +10,7 @@
 HEAD_DIM = 128
 BLOCK_ROWS = 128
 FRAMES = 4
+ROW = 8
 TILE = 128
 LOG2E = math.log2(math.e)
 MESH = pl.DeviceIdType.MESH
@@ -37,6 +38,8 @@
     back_sem,
     send_sem,
     local_sem,
+    relay_sem,
+    relayed,
 ):
     seq = lax.axis_index("seq")
     cam = lax.axis_index("cam")
@@ -47,6 +50,18 @@
     right = lax.rem(cam + 1, cams)
     blk = lax.div(seq * rows, BLOCK_ROWS)
 
+    place = lax.rem(cam, ROW)
+    row = cam - place
+    row_before = lax.rem(row + cams - ROW, cams)
+    row_after = lax.rem(row + ROW, cams)
+    is_first, is_last = place == 0, place == ROW - 1
+    hands_right, hands_left = place == 1, place == ROW - 2
+    hands_on = hands_right | hands_left
+    giver = jnp.where(hands_right, row + ROW - 1, row)
+    taker = jnp.where(hands_right, row_after, row_before + ROW - 1)
+    helper_out = jnp.where(is_last, row + 1, row + ROW - 2)
+    helper_in = jnp.where(is_last, row_after + ROW - 2, row_before + 1)
+
     barrier = pltpu.get_barrier_semaphore()
 
     def greet(i, carry):
@@ -58,7 +73,22 @@
     lax.fori_loop(1, peers, greet, 0)
     for other in (left, right):
         pl.semaphore_signal(barrier, inc=1, device_id={"cam": other}, device_id_type=MESH)
-    pl.semaphore_wait(barrier, peers + 1)
+
+    at_edge = is_first | is_last
+
+    def greet_two(one, two):
+        for other in (one, two):
+            pl.semaphore_signal(barrier, inc=1, device_id={"cam": other}, device_id_type=MESH)
+
+    @pl.when(hands_on)
+    def _():
+        greet_two(giver, taker)
+
+    @pl.when(at_edge)
+    def _():
+        greet_two(helper_out, helper_in)
+
+    pl.semaphore_wait(barrier, peers + 1 + jnp.where(hands_on | at_edge, 2, 0))
 
     sources = (k_hbm, v_hbm, q_hbm)
     places = (kv.at[0, 0], kv.at[1, 0], qb)
@@ -95,15 +125,44 @@
         pltpu.make_async_copy(places[a].at[f], places[a].at[f], in_sem.at[a, f]).wait()
 
     def forward(a, f):
-        for slot, other in ((1, right), (2, left)):
-            pltpu.make_async_remote_copy(
-                src_ref=kv.at[a, 0, f],
-                dst_ref=kv.at[a, slot, f],
-                send_sem=send_sem.at[3],
-                recv_sem=cam_sem.at[f],
-                device_id={"cam": other},
-                device_id_type=MESH,
-            ).start()
+        for slot, other, edge in ((1, right, is_last), (2, left, is_first)):
+
+            def send(dst_ref, recv_sem, device):
+                pltpu.make_async_remote_copy(
+                    src_ref=kv.at[a, 0, f],
+                    dst_ref=dst_ref,
+                    send_sem=send_sem.at[3],
+                    recv_sem=recv_sem,
+                    device_id={"cam": device},
+                    device_id_type=MESH,
+                ).start()
+
+            if a == 1:
+                send(kv.at[a, slot, f], cam_sem.at[f], other)
+            else:
+
+                @pl.when(edge)
+                def _():
+                    send(relayed.at[f], relay_sem.at[f], helper_out)
+
+                @pl.when(jnp.logical_not(edge))
+                def _():
+                    send(kv.at[a, slot, f], cam_sem.at[f], other)
+
+    def hand_on(f):
+        for slot, acts in ((1, hands_right), (2, hands_left)):
+
+            @pl.when(acts)
+            def _():
+                pltpu.make_async_copy(relayed.at[f], relayed.at[f], relay_sem.at[f]).wait()
+                pltpu.make_async_remote_copy(
+                    src_ref=relayed.at[f],
+                    dst_ref=kv.at[0, slot, f],
+                    send_sem=send_sem.at[5],
+                    recv_sem=cam_sem.at[f],
+                    device_id={"cam": taker},
+                    device_id_type=MESH,
+                ).start()
 
     scale = LOG2E / math.sqrt(HEAD_DIM)
     left_first = neighbours_ref[0, 0] == left
@@ -199,6 +258,7 @@
         forward(0, f)
         wait_in(1, f)
         forward(1, f)
+        hand_on(f)
         wait_in(2, f)
         if f + 2 < FRAMES:
             scatter(f + 2)
@@ -232,6 +292,11 @@
         pltpu.make_async_copy(sent, sent, send_sem.at[a]).wait()
     sent = kv.at[:, 1:3]
     pltpu.make_async_copy(sent, sent, send_sem.at[3]).wait()
+
+    @pl.when(hands_on)
+    def _():
+        pltpu.make_async_copy(relayed, relayed, send_sem.at[5]).wait()
+
     sent = ob.at[:, pl.ds(0, received)]
     pltpu.make_async_copy(sent, sent, send_sem.at[4]).wait()
 
@@ -267,8 +332,10 @@
             pltpu.SemaphoreType.DMA((3, frames)),
             pltpu.SemaphoreType.DMA((frames,)),
             pltpu.SemaphoreType.DMA((frames,)),
-            pltpu.SemaphoreType.DMA((5,)),
+            pltpu.SemaphoreType.DMA((6,)),
             pltpu.SemaphoreType.DMA((3,)),
+            pltpu.SemaphoreType.DMA((frames,)),
+            pltpu.VMEM((frames, positions, HEAD_DIM), dtype),
         ],
         compiler_params=pltpu.CompilerParams(
             collective_id=0, has_side_effects=True, vmem_limit_bytes=60 << 20

time: 76.8 us -> 69.5 us (0.905)
  Pallas kernels: 74.7 us -> 67.4 us
    pallas_call x1, Pallas kernels: 74.7 us -> 67.4 us  [local(): pl.pallas_call(kernel, out_shape=jax.ShapeDtypeStruct(cross_queries.shape...]
where the time goes in v2:
time: 69.5 us; the launch traced here: 69.3 us
  Pallas kernels  67.4 us (97%)
  local copies, waits for them, and re-layouts  1.88 us (3%)
    pallas_call x1, Pallas kernels, local(): pl.pallas_call(kernel, out_shape=jax.ShapeDtypeStruct(cross_queries.shape...  67.4 us
    unnamed x1, local copies, waits for them, and re-layouts  1.88 us

profile of v2, /device:TPU:64, one launch (start us, length us, event | category | flops | bytes accessed | tf_op | source)
XLA Modules:
  0.0 69.3 jit_solution(1576482390168035628)
XLA Ops:
  0.0 67.4 %shard_map.91 = bf16[1,4,32,2048]{3,2,1,0:T(8,128)(2,1)} custom-call(s32[1,4,4]{2,1,0:T(4,128)} %refresh_ref.1, s32[1,2]{1,0:T(1,128)} %neighbours_ref.1, f32[3,16]{1,0:T(4,128)} %bias_ref.1, bf16[1,4,32,2048]{3,2,1,0:T(8,128)(2,1)} %q_hbm.1, bf16[1,4,32,2048]{3,2,1,0:T(8,128)(2,1)} %k_hbm.1, bf16[1,4,32,2048]{3,2,1,0:T(8,128)(2,1)} %v_hbm.1, ...), custom_call_target="tpu_custom_call" | custom-call | tf_op jit(solution)/shard_map/pallas_call | solution.py:320
  67.4 1.9 %copy.11 = bf16[1,4,32,2048]{3,2,1,0:T(8,128)(2,1)} copy(bf16[1,4,32,2048]{3,2,1,0:T(8,128)(2,1)} %shard_map.91) | data formatting | bytes 1048576

commit v3 on v2

--- a/solution.py
+++ b/solution.py
@@ -55,12 +55,14 @@
     row_before = lax.rem(row + cams - ROW, cams)
     row_after = lax.rem(row + ROW, cams)
     is_first, is_last = place == 0, place == ROW - 1
-    hands_right, hands_left = place == 1, place == ROW - 2
+    is_edge = is_first | is_last
+    hands_right = (place == 1) | (place == 2)
+    hands_left = (place == ROW - 2) | (place == ROW - 3)
     hands_on = hands_right | hands_left
+    handed = jnp.where((place == 1) | (place == ROW - 2), 0, 1)
     giver = jnp.where(hands_right, row + ROW - 1, row)
     taker = jnp.where(hands_right, row_after, row_before + ROW - 1)
-    helper_out = jnp.where(is_last, row + 1, row + ROW - 2)
-    helper_in = jnp.where(is_last, row_after + ROW - 2, row_before + 1)
+    taker_slot = jnp.where(hands_right, 1, 2)
 
     barrier = pltpu.get_barrier_semaphore()
 
@@ -70,25 +72,34 @@
         )
         return carry
 
+    def greet_cam(other):
+        pl.semaphore_signal(barrier, inc=1, device_id={"cam": other}, device_id_type=MESH)
+
     lax.fori_loop(1, peers, greet, 0)
-    for other in (left, right):
-        pl.semaphore_signal(barrier, inc=1, device_id={"cam": other}, device_id_type=MESH)
-
-    at_edge = is_first | is_last
-
-    def greet_two(one, two):
-        for other in (one, two):
-            pl.semaphore_signal(barrier, inc=1, device_id={"cam": other}, device_id_type=MESH)
+
+    @pl.when(jnp.logical_not(is_last))
+    def _():
+        greet_cam(right)
+
+    @pl.when(jnp.logical_not(is_first))
+    def _():
+        greet_cam(left)
 
     @pl.when(hands_on)
     def _():
-        greet_two(giver, taker)
-
-    @pl.when(at_edge)
-    def _():
-        greet_two(helper_out, helper_in)
-
-    pl.semaphore_wait(barrier, peers + 1 + jnp.where(hands_on | at_edge, 2, 0))
+        greet_cam(giver)
+
+    @pl.when(is_first)
+    def _():
+        greet_cam(row_before + 1)
+        greet_cam(row_before + 2)
+
+    @pl.when(is_last)
+    def _():
+        greet_cam(row_after + ROW - 2)
+        greet_cam(row_after + ROW - 3)
+
+    pl.semaphore_wait(barrier, peers + 1 + jnp.where(is_edge | hands_on, 1, 0))
 
     sources = (k_hbm, v_hbm, q_hbm)
     places = (kv.at[0, 0], kv.at[1, 0], qb)
@@ -99,8 +110,8 @@
     def my_rows(index):
         return pl.ds(pl.multiple_of(index * rows, rows), rows)
 
-    def scatter(f):
-        for a in range(3):
+    def scatter(f, arrays):
+        for a in arrays:
 
             def send(i, carry):
                 peer = lax.rem(seq + i, peers)
@@ -125,7 +136,10 @@
         pltpu.make_async_copy(places[a].at[f], places[a].at[f], in_sem.at[a, f]).wait()
 
     def forward(a, f):
-        for slot, other, edge in ((1, right, is_last), (2, left, is_first)):
+        for slot, other, edge, helper in (
+            (1, right, is_last, row + 1 + a),
+            (2, left, is_first, row + ROW - 2 - a),
+        ):
 
             def send(dst_ref, recv_sem, device):
                 pltpu.make_async_remote_copy(
@@ -137,32 +151,26 @@
                     device_id_type=MESH,
                 ).start()
 
-            if a == 1:
+            @pl.when(edge)
+            def _():
+                send(relayed.at[f], relay_sem.at[f], helper)
+
+            @pl.when(jnp.logical_not(edge))
+            def _():
                 send(kv.at[a, slot, f], cam_sem.at[f], other)
-            else:
-
-                @pl.when(edge)
-                def _():
-                    send(relayed.at[f], relay_sem.at[f], helper_out)
-
-                @pl.when(jnp.logical_not(edge))
-                def _():
-                    send(kv.at[a, slot, f], cam_sem.at[f], other)
 
     def hand_on(f):
-        for slot, acts in ((1, hands_right), (2, hands_left)):
-
-            @pl.when(acts)
-            def _():
-                pltpu.make_async_copy(relayed.at[f], relayed.at[f], relay_sem.at[f]).wait()
-                pltpu.make_async_remote_copy(
-                    src_ref=relayed.at[f],
-                    dst_ref=kv.at[0, slot, f],
-                    send_sem=send_sem.at[5],
-                    recv_sem=cam_sem.at[f],
-                    device_id={"cam": taker},
-                    device_id_type=MESH,
-                ).start()
+        @pl.when(hands_on)
+        def _():
+            pltpu.make_async_copy(relayed.at[f], relayed.at[f], relay_sem.at[f]).wait()
+            pltpu.make_async_remote_copy(
+                src_ref=relayed.at[f],
+                dst_ref=kv.at[handed, taker_slot, f],
+                send_sem=send_sem.at[5],
+                recv_sem=cam_sem.at[f],
+                device_id={"cam": taker},
+                device_id_type=MESH,
+            ).start()
 
     scale = LOG2E / math.sqrt(HEAD_DIM)
     left_first = neighbours_ref[0, 0] == left
@@ -241,30 +249,31 @@
                 )
         return carry
 
-    scatter(0)
-    scatter(1)
+    for f in range(2):
+        scatter(f, (0, 1))
     own_rows = [
         pltpu.make_async_copy(src.at[0], local3.at[n], local_sem.at[n])
         for n, src in enumerate((cached_hbm, tq_hbm, tk_hbm))
     ]
     for copy in own_rows:
         copy.start()
-    for copy in own_rows:
-        copy.wait()
-    lax.fori_loop(0, peers, time_weights, 0)
-
     for f in range(FRAMES):
         wait_in(0, f)
         forward(0, f)
         wait_in(1, f)
         forward(1, f)
         hand_on(f)
+        if f + 2 < FRAMES:
+            scatter(f + 2, (0, 1))
+        else:
+            scatter(2 * f - 4, (2,))
+            scatter(2 * f - 3, (2,))
+    for copy in own_rows:
+        copy.wait()
+    lax.fori_loop(0, peers, time_weights, 0)
+    for f in range(FRAMES):
         wait_in(2, f)
-        if f + 2 < FRAMES:
-            scatter(f + 2)
-        if f > 0:
-            attend(f - 1)
-    attend(FRAMES - 1)
+        attend(f)
 
     for f in range(FRAMES):
         pltpu.make_async_copy(mix.at[f], mix.at[f], back_sem.at[f]).wait()

time: 69.5 us -> 65.7 us (0.945)
  Pallas kernels: 67.4 us -> 63.6 us
    pallas_call x1, Pallas kernels: 67.4 us -> 63.6 us  [local(): pl.pallas_call(kernel, out_shape=jax.ShapeDtypeStruct(cross_queries.shape...]
where the time goes in v3:
time: 65.7 us; the launch traced here: 65.5 us
  Pallas kernels  63.6 us (97%)
  local copies, waits for them, and re-layouts  1.88 us (3%)
    pallas_call x1, Pallas kernels, local(): pl.pallas_call(kernel, out_shape=jax.ShapeDtypeStruct(cross_queries.shape...  63.6 us
    unnamed x1, local copies, waits for them, and re-layouts  1.88 us

profile of v3, /device:TPU:64, one launch (start us, length us, event | category | flops | bytes accessed | tf_op | source)
XLA Modules:
  0.0 65.5 jit_solution(12345488246045721929)
XLA Ops:
  0.0 63.6 %shard_map.91 = bf16[1,4,32,2048]{3,2,1,0:T(8,128)(2,1)} custom-call(s32[1,4,4]{2,1,0:T(4,128)} %refresh_ref.1, s32[1,2]{1,0:T(1,128)} %neighbours_ref.1, f32[3,16]{1,0:T(4,128)} %bias_ref.1, bf16[1,4,32,2048]{3,2,1,0:T(8,128)(2,1)} %q_hbm.1, bf16[1,4,32,2048]{3,2,1,0:T(8,128)(2,1)} %k_hbm.1, bf16[1,4,32,2048]{3,2,1,0:T(8,128)(2,1)} %v_hbm.1, ...), custom_call_target="tpu_custom_call" | custom-call | tf_op jit(solution)/shard_map/pallas_call | solution.py:329
  63.6 1.9 %copy.11 = bf16[1,4,32,2048]{3,2,1,0:T(8,128)(2,1)} copy(bf16[1,4,32,2048]{3,2,1,0:T(8,128)(2,1)} %shard_map.91) | data formatting | bytes 1048576

commit v4 on v3

--- a/solution.py
+++ b/solution.py
@@ -11,7 +11,7 @@
 BLOCK_ROWS = 128
 FRAMES = 4
 ROW = 8
-TILE = 128
+TILE = 256
 LOG2E = math.log2(math.e)
 MESH = pl.DeviceIdType.MESH
 
@@ -40,6 +40,7 @@
     local_sem,
     relay_sem,
     relayed,
+    sums,
 ):
     seq = lax.axis_index("seq")
     cam = lax.axis_index("cam")
@@ -213,24 +214,32 @@
             ob[f, tile] = (acc / total).astype(jnp.bfloat16)
             return carry
 
-        lax.fori_loop(0, qb.shape[1] // TILE, tile_work, 0)
-
-        def give_back(i, carry):
-            peer = lax.rem(seq + i, peers)
-            pltpu.make_async_remote_copy(
-                src_ref=ob.at[f, my_rows(peer)],
-                dst_ref=mix.at[f, :, head_cols(seq)],
-                send_sem=send_sem.at[4],
-                recv_sem=back_sem.at[f],
-                device_id={"seq": peer},
-                device_id_type=MESH,
-            ).start()
+        def give_back(peer, carry):
+            @pl.when(peer != seq)
+            def _():
+                pltpu.make_async_remote_copy(
+                    src_ref=ob.at[f, my_rows(peer)],
+                    dst_ref=mix.at[f, :, head_cols(seq)],
+                    send_sem=send_sem.at[4],
+                    recv_sem=back_sem.at[f],
+                    device_id={"seq": peer},
+                    device_id_type=MESH,
+                ).start()
+
+            @pl.when(peer == seq)
+            def _():
+                pltpu.make_async_copy(
+                    ob.at[f, my_rows(seq)], mix.at[f, :, head_cols(seq)], back_sem.at[f]
+                ).start()
+
             return carry
 
-        lax.fori_loop(1, peers, give_back, 0)
-        pltpu.make_async_copy(
-            ob.at[f, my_rows(seq)], mix.at[f, :, head_cols(seq)], back_sem.at[f]
-        ).start()
+        def tile_and_send(t, carry):
+            tile_work(t, carry)
+            lax.fori_loop(t * (TILE // rows), (t + 1) * (TILE // rows), give_back, 0)
+            return carry
+
+        lax.fori_loop(0, qb.shape[1] // TILE, tile_and_send, 0)
 
     def time_weights(h, carry):
         cols = head_cols(h)
@@ -275,25 +284,42 @@
         wait_in(2, f)
         attend(f)
 
-    for f in range(FRAMES):
-        pltpu.make_async_copy(mix.at[f], mix.at[f], back_sem.at[f]).wait()
-
     flags = [refresh_ref[0, g, blk] == 1 for g in range(FRAMES)]
 
-    def combine(h, carry):
+    def wait_back(g):
+        pltpu.make_async_copy(mix.at[g], mix.at[g], back_sem.at[g]).wait()
+
+    def mixed(g, cols):
+        return jnp.where(flags[g], mix[g, :, cols], local3[0, g, :, cols]).astype(jnp.float32)
+
+    def term(f, g, cols, value):
+        return weights[f, g, :, cols].astype(jnp.float32) * value
+
+    for g in range(FRAMES - 1):
+        wait_back(g)
+
+    def combine_first(h, carry):
         cols = head_cols(h)
-        mixed = [
-            jnp.where(flags[g], mix[g, :, cols], local3[0, g, :, cols]).astype(jnp.float32)
-            for g in range(FRAMES)
-        ]
+        values = [mixed(g, cols) for g in range(FRAMES - 1)]
         for f in range(FRAMES):
-            acc = weights[f, 0, :, cols].astype(jnp.float32) * mixed[0]
-            for g in range(1, FRAMES):
-                acc = acc + weights[f, g, :, cols].astype(jnp.float32) * mixed[g]
+            acc = term(f, 0, cols, values[0])
+            for g in range(1, FRAMES - 1):
+                acc = acc + term(f, g, cols, values[g])
+            sums[f, :, cols] = acc
+        return carry
+
+    lax.fori_loop(0, peers, combine_first, 0)
+    wait_back(FRAMES - 1)
+
+    def combine_last(h, carry):
+        cols = head_cols(h)
+        value = mixed(FRAMES - 1, cols)
+        for f in range(FRAMES):
+            acc = sums[f, :, cols] + term(f, FRAMES - 1, cols, value)
             out_ref[0, f, :, cols] = acc.astype(jnp.bfloat16)
         return carry
 
-    lax.fori_loop(0, peers, combine, 0)
+    lax.fori_loop(0, peers, combine_last, 0)
 
     received = qb.shape[1] - rows
     for a in range(3):
@@ -328,7 +354,7 @@
     hbm = pl.BlockSpec(memory_space=pltpu.HBM)
     return pl.pallas_call(
         kernel,
-        out_shape=jax.ShapeDtypeStruct(cross_queries.shape, dtype),
+        out_shape=pltpu.VMEM(cross_queries.shape, dtype),
         in_specs=[smem] * 3 + [hbm] * 6,
         out_specs=pl.BlockSpec(memory_space=pltpu.VMEM),
         scratch_shapes=[
@@ -345,6 +371,7 @@
             pltpu.SemaphoreType.DMA((3,)),
             pltpu.SemaphoreType.DMA((frames,)),
             pltpu.VMEM((frames, positions, HEAD_DIM), dtype),
+            pltpu.VMEM((frames, rows, inner), jnp.float32),
         ],
         compiler_params=pltpu.CompilerParams(
             collective_id=0, has_side_effects=True, vmem_limit_bytes=60 << 20
@@ -353,12 +380,12 @@
         refresh,
         neighbours,
         view_bias,
-        cross_queries,
-        cross_keys,
-        cross_values,
-        cached_cross,
-        time_queries,
-        time_keys,
+        pltpu.with_memory_space_constraint(cross_queries, pltpu.HBM),
+        pltpu.with_memory_space_constraint(cross_keys, pltpu.HBM),
+        pltpu.with_memory_space_constraint(cross_values, pltpu.HBM),
+        pltpu.with_memory_space_constraint(cached_cross, pltpu.HBM),
+        pltpu.with_memory_space_constraint(time_queries, pltpu.HBM),
+        pltpu.with_memory_space_constraint(time_keys, pltpu.HBM),
     )
 
 

time: 65.7 us -> 60.9 us (0.927)
  Pallas kernels: 63.6 us -> 59.9 us
  local copies, waits for them, and re-layouts: 1.88 us -> 0.8 us
    pallas_call x1, Pallas kernels: 63.6 us -> 59.9 us  [local(): pl.pallas_call(kernel, out_shape=pltpu.VMEM(cross_queries.shape, dtype),...]
    unnamed x1, local copies, waits for them, and re-layouts: 1.88 us -> 0.8 us
where the time goes in v4:
time: 60.9 us; the launch traced here: 60.7 us
  Pallas kernels  59.9 us (98%)
  local copies, waits for them, and re-layouts  0.8 us (1%)
    pallas_call x1, Pallas kernels, local(): pl.pallas_call(kernel, out_shape=pltpu.VMEM(cross_queries.shape, dtype),...  59.9 us

profile of v4, /device:TPU:64, one launch (start us, length us, event | category | flops | bytes accessed | tf_op | source)
XLA Modules:
  0.0 60.7 jit_solution(13452483965392582813)
XLA Ops:
  0.0 59.9 %shard_map.91 = bf16[1,4,32,2048]{3,2,1,0:T(8,128)(2,1)S(1)} custom-call(s32[1,4,4]{2,1,0:T(4,128)} %refresh_ref.1, s32[1,2]{1,0:T(1,128)} %neighbours_ref.1, f32[3,16]{1,0:T(4,128)} %bias_ref.1, bf16[1,4,32,2048]{3,2,1,0:T(8,128)(2,1)} %q_hbm.1, bf16[1,4,32,2048]{3,2,1,0:T(8,128)(2,1)} %k_hbm.1, bf16[1,4,32,2048]{3,2,1,0:T(8,128)(2,1)} %v_hbm.1, ...), custom_call_target="tpu_custom_call" | custom-call | tf_op jit(solution)/shard_map/pallas_call | solution.py:355
  59.9 0.8 %copy.11 = bf16[1,4,32,2048]{3,2,1,0:T(8,128)(2,1)} copy(bf16[1,4,32,2048]{3,2,1,0:T(8,128)(2,1)S(1)} %shard_map.91) | data formatting | bytes 1048576

commit v5 on v4

--- a/solution.py
+++ b/solution.py
@@ -17,9 +17,9 @@
 
 
 def kernel(
-    refresh_ref,
-    neighbours_ref,
-    bias_ref,
+    refresh_hbm,
+    neighbours_hbm,
+    bias_hbm,
     q_hbm,
     k_hbm,
     v_hbm,
@@ -40,6 +40,9 @@
     local_sem,
     relay_sem,
     relayed,
+    refresh_ref,
+    neighbours_ref,
+    bias_ref,
     sums,
 ):
     seq = lax.axis_index("seq")
@@ -160,8 +163,8 @@
             def _():
                 send(kv.at[a, slot, f], cam_sem.at[f], other)
 
-    def hand_on(f):
-        @pl.when(hands_on)
+    def hand_on(f, kind):
+        @pl.when(hands_on & (handed == kind))
         def _():
             pltpu.make_async_copy(relayed.at[f], relayed.at[f], relay_sem.at[f]).wait()
             pltpu.make_async_remote_copy(
@@ -172,17 +175,6 @@
                 device_id={"cam": taker},
                 device_id_type=MESH,
             ).start()
-
-    scale = LOG2E / math.sqrt(HEAD_DIM)
-    left_first = neighbours_ref[0, 0] == left
-    bias_own = bias_ref[0, seq] * LOG2E
-    bias_a = bias_ref[1, seq] * LOG2E
-    bias_b = bias_ref[2, seq] * LOG2E
-    biases = (
-        bias_own,
-        jnp.where(left_first, bias_a, bias_b),
-        jnp.where(left_first, bias_b, bias_a),
-    )
 
     def attend(f):
         pltpu.make_async_copy(kv.at[:, 1:3, f], kv.at[:, 1:3, f], cam_sem.at[f]).wait()
@@ -260,23 +252,48 @@
 
     for f in range(2):
         scatter(f, (0, 1))
+    small = [
+        pltpu.make_async_copy(src, dst, local_sem.at[3 + n])
+        for n, (src, dst) in enumerate(
+            ((refresh_hbm, refresh_ref), (neighbours_hbm, neighbours_ref), (bias_hbm, bias_ref))
+        )
+    ]
+    for copy in small:
+        copy.start()
     own_rows = [
         pltpu.make_async_copy(src.at[0], local3.at[n], local_sem.at[n])
         for n, src in enumerate((cached_hbm, tq_hbm, tk_hbm))
     ]
     for copy in own_rows:
         copy.start()
+    for copy in small:
+        copy.wait()
+
+    scale = LOG2E / math.sqrt(HEAD_DIM)
+    left_first = neighbours_ref[0, 0] == left
+    bias_own = bias_ref[0, seq] * LOG2E
+    bias_a = bias_ref[1, seq] * LOG2E
+    bias_b = bias_ref[2, seq] * LOG2E
+    biases = (
+        bias_own,
+        jnp.where(left_first, bias_a, bias_b),
+        jnp.where(left_first, bias_b, bias_a),
+    )
+
     for f in range(FRAMES):
         wait_in(0, f)
         forward(0, f)
+        if f > 0:
+            hand_on(f - 1, 1)
         wait_in(1, f)
         forward(1, f)
-        hand_on(f)
+        hand_on(f, 0)
         if f + 2 < FRAMES:
             scatter(f + 2, (0, 1))
         else:
             scatter(2 * f - 4, (2,))
             scatter(2 * f - 3, (2,))
+    hand_on(FRAMES - 1, 1)
     for copy in own_rows:
         copy.wait()
     lax.fori_loop(0, peers, time_weights, 0)
@@ -350,12 +367,11 @@
     _, frames, rows, inner = cross_queries.shape
     positions = rows * lax.axis_size("seq")
     dtype = jnp.bfloat16
-    smem = pl.BlockSpec(memory_space=pltpu.SMEM)
     hbm = pl.BlockSpec(memory_space=pltpu.HBM)
     return pl.pallas_call(
         kernel,
         out_shape=pltpu.VMEM(cross_queries.shape, dtype),
-        in_specs=[smem] * 3 + [hbm] * 6,
+        in_specs=[hbm] * 9,
         out_specs=pl.BlockSpec(memory_space=pltpu.VMEM),
         scratch_shapes=[
             pltpu.VMEM((2, 3, frames, positions, HEAD_DIM), dtype),
@@ -368,18 +384,21 @@
             pltpu.SemaphoreType.DMA((frames,)),
             pltpu.SemaphoreType.DMA((frames,)),
             pltpu.SemaphoreType.DMA((6,)),
-            pltpu.SemaphoreType.DMA((3,)),
+            pltpu.SemaphoreType.DMA((6,)),
             pltpu.SemaphoreType.DMA((frames,)),
             pltpu.VMEM((frames, positions, HEAD_DIM), dtype),
+            pltpu.SMEM(refresh.shape, refresh.dtype),
+            pltpu.SMEM(neighbours.shape, neighbours.dtype),
+            pltpu.SMEM(view_bias.shape, view_bias.dtype),
             pltpu.VMEM((frames, rows, inner), jnp.float32),
         ],
         compiler_params=pltpu.CompilerParams(
             collective_id=0, has_side_effects=True, vmem_limit_bytes=60 << 20
         ),
     )(
-        refresh,
-        neighbours,
-        view_bias,
+        pltpu.with_memory_space_constraint(refresh, pltpu.HBM),
+        pltpu.with_memory_space_constraint(neighbours, pltpu.HBM),
+        pltpu.with_memory_space_constraint(view_bias, pltpu.HBM),
         pltpu.with_memory_space_constraint(cross_queries, pltpu.HBM),
         pltpu.with_memory_space_constraint(cross_keys, pltpu.HBM),
         pltpu.with_memory_space_constraint(cross_values, pltpu.HBM),

time: 60.9 us -> 60.5 us (level)
  no operation moved by 1% of the time
where the time goes in v5:
time: 60.5 us; the launch traced here: 60.4 us
  Pallas kernels  59.6 us (99%)
  local copies, waits for them, and re-layouts  0.8 us (1%)
    pallas_call x1, Pallas kernels, local(): pl.pallas_call(kernel, out_shape=pltpu.VMEM(cross_queries.shape, dtype),...  59.6 us

profile of v5, /device:TPU:64, one launch (start us, length us, event | category | flops | bytes accessed | tf_op | source)
XLA Modules:
  0.0 60.4 jit_solution(3407154233810669187)
XLA Ops:
  0.0 59.6 %shard_map.91 = bf16[1,4,32,2048]{3,2,1,0:T(8,128)(2,1)S(1)} custom-call(s32[1,4,4]{2,1,0:T(4,128)} %refresh_hbm.1, s32[1,2]{1,0:T(1,128)} %neighbours_hbm.1, f32[3,16]{1,0:T(4,128)} %bias_hbm.1, bf16[1,4,32,2048]{3,2,1,0:T(8,128)(2,1)} %q_hbm.1, bf16[1,4,32,2048]{3,2,1,0:T(8,128)(2,1)} %k_hbm.1, bf16[1,4,32,2048]{3,2,1,0:T(8,128)(2,1)} %v_hbm.1, ...), custom_call_target="tpu_custom_call" | custom-call | tf_op jit(solution)/shard_map/pallas_call | solution.py:371
  59.6 0.8 %copy.11 = bf16[1,4,32,2048]{3,2,1,0:T(8,128)(2,1)} copy(bf16[1,4,32,2048]{3,2,1,0:T(8,128)(2,1)S(1)} %shard_map.91) | data formatting | bytes 1048576
